TPU v7x, 512 devices: a whole 4x4x16 slice. The times are simulated.
512 devices in a mesh: row: 64 (over y, z), col: 8 (over x, core).
Axes of the slice: x: 4, y: 4, z: 16, core: 2. Of those that a mesh axis runs over, the one named last changes fastest.
Arguments:
- activations: bfloat16 [512, 8192], P('row', 'col'), may hold values from -6 to 6
- gate_weight: bfloat16 [8192, 16384], P('col', 'row'), may hold values from -0.0625 to 0.0625
- up_weight: bfloat16 [8192, 16384], P('col', 'row'), may hold values from -0.0625 to 0.0625
- down_weight: bfloat16 [16384, 8192], P('row', 'col'), may hold values from -0.046875 to 0.046875
- out_grad: bfloat16 [512, 8192], P('row', 'col'), may hold values from -2.390625 to 2.390625
Outputs:
- grad_input: float32 [512, 8192], P('row', 'col')
- grad_gate_weight: bfloat16 [8192, 16384], P('col', 'row')
- grad_up_weight: bfloat16 [8192, 16384], P('col', 'row')
- grad_down_weight: bfloat16 [16384, 8192], P('row', 'col')
All inputs are finite; a program needn't handle non-finite values.
Results may differ from a plain program's by a relative error of at most 0.0049.
Values may be sent and summed in bfloat16 or wider, within the bound.
A program may use at most 64 MiB of HBM per device.

v0:
```python
import jax
import jax.numpy as jnp
from jax import lax
from jax.sharding import PartitionSpec as P


def forward_act(pre_gate, pre_up):
    sigma = jax.nn.sigmoid(pre_gate)
    return (pre_gate * sigma * pre_up).astype(jnp.bfloat16)


def backward_act(grad_hidden, pre_gate, pre_up):
    sigma = jax.nn.sigmoid(pre_gate)
    grad_gate = (grad_hidden * pre_up * sigma * (1.0 + pre_gate * (1.0 - sigma))).astype(
        jnp.bfloat16
    )
    grad_up = (grad_hidden * (pre_gate * sigma)).astype(jnp.bfloat16)
    return (grad_gate, grad_up)


def contract_rows(left, right):
    return lax.dot_general(
        left, right, (((0,), (0,)), ((), ())), preferred_element_type=jnp.float32
    )


def contract_cols(left, right):
    return lax.dot_general(
        left, right, (((1,), (1,)), ((), ())), preferred_element_type=jnp.float32
    )


def on_device(activations, gate_weight, up_weight, down_weight, out_grad):
    input_cols = lax.all_gather(activations, "row", axis=0, tiled=True)
    gate_part = jnp.dot(input_cols, gate_weight, preferred_element_type=jnp.float32)
    up_part = jnp.dot(input_cols, up_weight, preferred_element_type=jnp.float32)
    pre_gate, pre_up = lax.psum((gate_part, up_part), "col")
    hidden = forward_act(pre_gate, pre_up)
    grad_cols = lax.all_gather(out_grad, "row", axis=0, tiled=True)
    hidden_part = contract_cols(grad_cols, down_weight)
    grad_down_weight = contract_rows(hidden, grad_cols).astype(jnp.bfloat16)
    grad_hidden = lax.psum(hidden_part, "col")
    grad_gate, grad_up = backward_act(grad_hidden, pre_gate, pre_up)
    grad_gate_weight = contract_rows(input_cols, grad_gate).astype(jnp.bfloat16)
    grad_up_weight = contract_rows(input_cols, grad_up).astype(jnp.bfloat16)
    grad_input = lax.psum_scatter(
        contract_cols(grad_gate, gate_weight) + contract_cols(grad_up, up_weight),
        "row",
        scatter_dimension=0,
        tiled=True,
    )
    return (grad_input, grad_gate_weight, grad_up_weight, grad_down_weight)


def solution(mesh):
    placed = (P("row", "col"), P("col", "row"), P("col", "row"), P("row", "col"), P("row", "col"))
    return jax.shard_map(
        on_device,
        mesh=mesh,
        in_specs=placed,
        out_specs=(P("row", "col"), P("col", "row"), P("col", "row"), P("row", "col")),
        check_vma=False,
    )
```

profile of v0, /device:TPU:6, one launch (start us, length us, event | category | flops | bytes accessed | tf_op | source)
XLA Modules:
  0.0 1077.0 jit_solution(17417460909710378519)
XLA Ops:
  7.2 0.0 copy-start
  7.2 0.0 copy-start.2
  7.2 0.0 all-gather.5.cloned.1.call-start
  7.2 0.7 all-gather.5.cloned.1.call-update
  7.9 0.0 all-gather.3.cloned.1.call-start
  8.0 0.7 all-gather.3.cloned.1.call-update
  8.7 0.0 copy-start.4
  8.7 0.0 all-reduce.3.cloned.1.call-start
  8.7 145.6 %all-gather.5.cloned.1.call-done = bf16[512,1024]{1,0:T(8,128)(2,1)} async-done(((bf16[8,1024]{1,0:T(8,128)(2,1)}), bf16[512,1024]{1,0:T(8,128)(2,1)}) %all-gather.5.cloned.1.call-update) | async-done | bytes 1048592 | tf_op jit(solution)/shard_map/all_gather | solution.py:34
  154.4 0.0 copy-done
  154.4 0.0 copy-start.1
  154.4 2.5 fusion.7
  156.9 0.0 copy-done.2
  156.9 0.0 copy-done.1
  156.9 1.2 fusion.6
  158.2 134.2 %all-gather.3.cloned.1.call-done = bf16[512,1024]{1,0:T(8,128)(2,1)} async-done(((bf16[8,1024]{1,0:T(8,128)(2,1)}), bf16[512,1024]{1,0:T(8,128)(2,1)}) %all-gather.3.cloned.1.call-update) | async-done | bytes 1048592 | tf_op jit(solution)/shard_map/all_gather | solution.py:39
  292.4 0.0 copy-done.4
  292.4 2.5 fusion.5
  294.9 0.0 all-reduce.3.cloned.1.call-update
  294.9 0.0 reduce-scatter.2.cloned.1.call-start
  295.0 73.9 %all-reduce.3.cloned.1.call-done = (f32[512,256]{1,0:T(8,128)}, f32[512,256]{1,0:T(8,128)}, f32[512,256]{1,0:T(8,128)}) async-done(((f32[512,256]{1,0:T(8,128)}, f32[512,256]{1,0:T(8,128)}, f32[512,256]{1,0:T(8,128)}), (f32[512,256]{1,0:T(8,128)}, f32[512,256]{1,0:T(8,128)}, f32[512,256]{1,0:T(8,128)})) %all-reduce.3.cloned.1.call-update) | async-done | bytes 1572880 | tf_op jit(solution)/shard_map/psum | solution.py:37
  368.8 1.6 multiply_convert_fusion.1
  370.5 0.5 fusion.8
  370.9 1.8 convolution_add_fusion
  372.7 0.0 reduce-scatter.2.cloned.1.call-update
  372.8 0.5 fusion
  373.2 0.0 copy-start.3
  373.2 1.0 copy.9
  374.2 0.5 fusion.1
  374.7 1.0 copy.10
  375.7 0.0 copy-done.3
  375.7 2.5 convolution_convert_fusion
  378.2 692.2 %reduce-scatter.2.cloned.1.call-done = f32[8,1024]{1,0:T(8,128)} async-done(((f32[512,1024]{1,0:T(8,128)}), f32[8,1024]{1,0:T(8,128)}) %reduce-scatter.2.cloned.1.call-update) | async-done | bytes 32784 | tf_op jit(solution)/shard_map/reduce_scatter | solution.py:46
Async XLA Ops:
  7.2 147.2 %copy-start = (bf16[1024,256]{1,0:T(8,128)(2,1)S(1)}, bf16[1024,256]{1,0:T(8,128)(2,1)}, u32[]{:S(2)}) copy-start(bf16[1024,256]{1,0:T(8,128)(2,1)} %param.6) | copy-start | bytes 1572868
  7.2 149.8 %copy-start.2 = (bf16[1024,256]{1,0:T(8,128)(2,1)S(1)}, bf16[1024,256]{1,0:T(8,128)(2,1)}, u32[]{:S(2)}) copy-start(bf16[1024,256]{1,0:T(8,128)(2,1)} %param.7) | copy-start | bytes 1572868
  7.2 147.2 %all-gather.5.cloned.1.call-start = ((), (), s32[]{:S(2)}) async-start(), calls=%async_computation.2 | async-start | bytes 1064960 | tf_op jit(solution)/shard_map/all_gather | solution.py:34
  7.9 284.5 %all-gather.3.cloned.1.call-start = ((), (), s32[]{:S(2)}) async-start(), calls=%async_computation.1 | async-start | bytes 1064960 | tf_op jit(solution)/shard_map/all_gather | solution.py:39
  8.7 283.7 %copy-start.4 = (bf16[256,1024]{1,0:T(8,128)(2,1)S(1)}, bf16[256,1024]{1,0:T(8,128)(2,1)}, u32[]{:S(2)}) copy-start(bf16[256,1024]{1,0:T(8,128)(2,1)} %param.8) | copy-start | bytes 1572868
  8.7 360.2 %all-reduce.3.cloned.1.call-start = ((), (), s32[]{:S(2)}) async-start(), calls=%async_computation.4 | async-start | bytes 3145728 | tf_op jit(solution)/shard_map/psum | solution.py:37
  154.4 2.6 copy-start.1
  294.9 775.5 %reduce-scatter.2.cloned.1.call-start = ((), (), s32[]{:S(2)}) async-start(), calls=%async_computation.3 | async-start | bytes 2129920 | tf_op jit(solution)/shard_map/reduce_scatter | solution.py:46
  373.2 2.5 copy-start.3
Sparse Core Ops, SparseCore 0:
  11.0 143.3 all-gather.4
  157.3 135.0 all-gather.2
  295.5 73.2 all-reduce.2
  373.7 696.7 reduce-scatter.1
where the time goes:
time: 1080 us
  waiting for transfers between devices  1050 us (97%)
  between operations  13.8 us (1%)
  matrix products  12 us (1%)
    reduce_scatter x1, waiting for transfers between devices, on_device(): lax.psum_scatter(contract_cols(grad_gate, gate_weight) + contract_cols(gr...  692 us
    all_gather x1, waiting for transfers between devices, on_device(): input_cols = lax.all_gather(activations, 'row', axis=0, tiled=True)  146 us
    all_gather x1, waiting for transfers between devices, on_device(): grad_cols = lax.all_gather(out_grad, 'row', axis=0, tiled=True)  134 us
    psum x1, waiting for transfers between devices, on_device(): pre_gate, pre_up = lax.psum((gate_part, up_part), 'col')  73.9 us
  transfers between devices with their start and end apart: 4, of which 4 were waited for; matrix products, arithmetic and copies ran while one was open for 1% of the time, Pallas kernels for 0%

commit v1 on v0

v1 whole, which is shorter than its diff:
```python
import functools

import jax
import jax.numpy as jnp
from jax import lax
from jax.experimental import pallas as pl
from jax.experimental.pallas import tpu as pltpu
from jax.sharding import PartitionSpec as P

MESH = pl.DeviceIdType.MESH
F32, BF16 = jnp.float32, jnp.bfloat16
NY, NZ, NX, NC = 4, 16, 4, 2
TOK, HID, FEAT = 8, 256, 1024
GROUP = NY * NZ * TOK // (NX * NC)

OWN = 2


def contract_cols(left, right):
    return lax.dot_general(left, right, (((1,), (1,)), ((), ())), preferred_element_type=F32)


def contract_rows(left, right):
    return lax.dot_general(left, right, (((0,), (0,)), ((), ())), preferred_element_type=F32)


def kernel(
    x_in, wg_in, wu_in, wd_in, dy_in,
    gi_out, gw_out, uw_out, dw_out,
    xf, df, xm, dm, w2, wd,
    p2, r1, s2, r2, pd, r1d, sd, r2d,
    h_all, g_all,
    gs, yr, acc, nb, nra, nrb, nrc, cs, cr,
    gw2, dwd,
    send_sem, recv_sem, load_sem,
):
    row, col = lax.axis_index("row"), lax.axis_index("col")
    y, z = row // NZ, row % NZ
    x, c = col // NC, col % NC
    o = 1 - c

    def at(dy=0, dz=0, dx=0):
        return (
            ((y + dy + NY) % NY) * NZ + (z + dz + NZ) % NZ,
            ((x + dx + NX) % NX) * NC + c,
        )

    other = (row, x * NC + o)

    loads = []

    def load(src, dst):
        copy = pltpu.make_async_copy(src, dst, load_sem.at[len(loads)])
        copy.start()
        loads.append(copy)
        return copy

    own = [load(x_in, xf.at[0, OWN]), load(dy_in, df.at[0, OWN])]
    weights = [
        load(wg_in, w2.at[:, pl.ds(0, HID)]),
        load(wu_in, w2.at[:, pl.ds(HID, HID)]),
        load(wd_in, wd),
    ]

    peers = [at(dz=k) for k in (1, -1, 2, -2, 3, -3)]
    peers += [at(dy=k) for k in (1, -1, 2)] + [at(dx=k) for k in (1, -1, 2)] + [other]
    barrier = pltpu.get_barrier_semaphore()
    for peer in peers:
        pl.semaphore_signal(barrier, inc=1, device_id=peer, device_id_type=MESH)
    for copy in own:
        copy.wait()
    pl.semaphore_wait(barrier, len(peers))

    sent = []

    def send(src, dst, to):
        i = len(sent)
        copy = pltpu.make_async_remote_copy(
            src_ref=src, dst_ref=dst, send_sem=send_sem.at[i], recv_sem=recv_sem.at[i],
            device_id=to, device_id_type=MESH,
        )
        copy.start()
        sent.append(copy)
        return copy

    def arrived(copies):
        for copy in copies:
            copy.wait_recv()

    y_of_x = []

    def spread_y(slots):
        for k in (2, 1, 3):
            y_of_x.append(send(xf.at[0, slots], xf.at[NY - k, slots], at(dy=k)))

    def one(i):
        return pl.ds(i, 1)

    xc1 = [send(xf.at[0, one(2)], xf.at[0, one(1)], at(dz=3)), send(xf.at[0, one(2)], xf.at[0, one(3)], at(dz=-3))]
    dyy = [send(df.at[0, one(2)], df.at[NY - k, one(2)], at(dy=k)) for k in (2, 1, 3)]
    spread_y(one(2))
    arrived(xc1)
    xc2 = [send(xf.at[0, one(1)], xf.at[0, one(0)], at(dz=3)), send(xf.at[0, one(3)], xf.at[0, one(4)], at(dz=-3))]
    arrived(dyy)
    dc1 = [send(df.at[:, one(2)], df.at[:, one(1)], at(dz=3)), send(df.at[:, one(2)], df.at[:, one(3)], at(dz=-3))]
    spread_y(one(1))
    spread_y(one(3))
    arrived(xc2)
    xn = [
        send(xf.at[0, pl.ds(0, 5)], xf.at[0, pl.ds(5, 5)], at(dz=1)),
        send(xf.at[0, pl.ds(0, 5)], xf.at[0, pl.ds(10, 5)], at(dz=-1)),
        send(xf.at[0, one(4)], xf.at[0, one(15)], at(dz=-2)),
    ]
    spread_y(one(0))
    spread_y(one(4))
    arrived(dc1)
    dc2 = [send(df.at[:, one(1)], df.at[:, one(0)], at(dz=3)), send(df.at[:, one(3)], df.at[:, one(4)], at(dz=-3))]
    arrived(xn)
    spread_y(pl.ds(5, 5))
    spread_y(pl.ds(10, 5))
    spread_y(one(15))
    arrived(dc2)
    dn = [
        send(df.at[:, pl.ds(0, 5)], df.at[:, pl.ds(5, 5)], at(dz=1)),
        send(df.at[:, pl.ds(0, 5)], df.at[:, pl.ds(10, 5)], at(dz=-1)),
        send(df.at[:, one(4)], df.at[:, one(15)], at(dz=-2)),
    ]
    for copy in weights:
        copy.wait()

    def compact(src, dst):
        def body(i, carry):
            slab = src[i // 4, pl.ds((i % 4) * 4, 4)].astype(F32).reshape(4 * TOK, FEAT)
            dst[pl.ds(pl.multiple_of(i * 32, 32), 32), :] = slab.astype(BF16)
            return carry

        lax.fori_loop(0, 16, body, 0)

    def reduce_parts(tokens, weight, product, part, r1, s, r2):
        first, second = [], []
        for k in (2, 1, 3, 0):
            m = (x + k) % NX
            rows = tokens[pl.ds(pl.multiple_of(m * 2 * GROUP, 2 * GROUP), 2 * GROUP), :]
            part[m] = product(rows, weight[...]).reshape(2, GROUP, part.shape[-1])
            first.append(send(part.at[m, o], r1.at[k], other))
        for k, copy in zip((2, 1, 3, 0), first):
            copy.wait_recv()
            s[k] = part[(x + k) % NX, c] + r1[k]
            if k:
                second.append(send(s.at[k], r2.at[k], at(dx=k)))
        return second

    arrived(y_of_x)
    compact(xf, xm)
    in2 = reduce_parts(xm, w2, lambda a, b: jnp.dot(a, b, preferred_element_type=F32), p2, r1, s2, r2)
    arrived(dn)
    compact(df, dm)
    ind = reduce_parts(dm, wd, contract_cols, pd, r1d, sd, r2d)

    arrived(in2)
    pre = s2[0] + r2[1] + r2[2] + r2[3]
    pre_gate, pre_up = pre[:, :HID], pre[:, HID:]
    sigma = jax.nn.sigmoid(pre_gate)
    silu = pre_gate * sigma
    h_all[x, c] = (silu * pre_up).astype(BF16)
    hx = [send(h_all.at[x, c], h_all.at[x, c], at(dx=k)) for k in (2, 1, 3)]
    hc = [send(h_all.at[x, c], h_all.at[x, c], other)]

    arrived(ind)
    grad_hidden = sd[0] + r2d[1] + r2d[2] + r2d[3]
    g_all[x, c, :, pl.ds(0, HID)] = (grad_hidden * pre_up * sigma * (1.0 + pre_gate * (1.0 - sigma))).astype(BF16)
    g_all[x, c, :, pl.ds(HID, HID)] = (grad_hidden * silu).astype(BF16)
    gx = [send(g_all.at[x, c], g_all.at[x, c], at(dx=k)) for k in (2, 1, 3)]
    gc = [send(g_all.at[x, c], g_all.at[x, c], other)]

    def pass_on(copies, array, to_other):
        for k, copy in zip((2, 1, 3), copies):
            copy.wait_recv()
            block = array.at[(x - k + NX) % NX, c]
            to_other.append(send(block, block, other))

    pass_on(hx, h_all, hc)
    pass_on(gx, g_all, gc)
    arrived(gc)

    def input_grad(m):
        return contract_cols(g_all[m].reshape(2 * GROUP, 2 * HID), w2[...])

    ys = []
    for k in (2, 1, 3):
        gs[k] = input_grad(k).astype(BF16)
        ys.append(send(gs.at[k], yr.at[k], at(dy=k)))
    acc[...] = input_grad(0)

    outs = []
    arrived(hc)
    dwd[...] = contract_rows(h_all[...].reshape(8 * GROUP, HID), dm[...]).astype(BF16)
    outs.append(load(dwd, dw_out))
    gw2[...] = contract_rows(xm[...], g_all[...].reshape(8 * GROUP, 2 * HID)).astype(BF16)
    outs.append(load(gw2.at[:, pl.ds(0, HID)], gw_out))
    outs.append(load(gw2.at[:, pl.ds(HID, HID)], uw_out))

    arrived(ys)
    total = acc[...] + yr[1].astype(F32) + yr[2].astype(F32) + yr[3].astype(F32)
    acc[...] = total
    nb[...] = total[5 * TOK :].reshape(11, TOK, FEAT).astype(BF16)
    near = [
        send(nb.at[pl.ds(0, 5)], nra, at(dz=-1)),
        send(nb.at[pl.ds(5, 5)], nrb, at(dz=1)),
        send(nb.at[pl.ds(10, 1)], nrc, at(dz=2)),
    ]
    arrived(near)

    def slot(i):
        value = acc[pl.ds(i * TOK, TOK), :] + nra[i].astype(F32) + nrb[i].astype(F32)
        return value + nrc[0].astype(F32) if i == 4 else value

    cs[0] = slot(4).astype(BF16)
    cs[1] = slot(0).astype(BF16)
    far = [send(cs.at[0], cr.at[0], at(dz=3)), send(cs.at[1], cr.at[1], at(dz=-3))]
    arrived(far)
    cs[2] = (slot(3) + cr[0].astype(F32)).astype(BF16)
    cs[3] = (slot(1) + cr[1].astype(F32)).astype(BF16)
    last = [send(cs.at[2], cr.at[2], at(dz=3)), send(cs.at[3], cr.at[3], at(dz=-3))]
    arrived(last)
    gi_out[...] = slot(2) + cr[2].astype(F32) + cr[3].astype(F32)

    for copy in outs:
        copy.wait()
    for copy in sent:
        copy.wait_send()


N_SENDS = 80
N_LOADS = 8


def on_device(activations, gate_weight, up_weight, down_weight, out_grad):
    hbm = pl.BlockSpec(memory_space=pl.ANY)
    vmem = pl.BlockSpec(memory_space=pltpu.VMEM)
    grad_input, grad_gate, grad_up, grad_down = pl.pallas_call(
        kernel,
        out_shape=(
            jax.ShapeDtypeStruct((TOK, FEAT), F32),
            jax.ShapeDtypeStruct((FEAT, HID), BF16),
            jax.ShapeDtypeStruct((FEAT, HID), BF16),
            jax.ShapeDtypeStruct((HID, FEAT), BF16),
        ),
        in_specs=[hbm] * 5,
        out_specs=(vmem, hbm, hbm, hbm),
        scratch_shapes=[
            pltpu.VMEM((NY, NZ, TOK, FEAT), BF16),
            pltpu.VMEM((NY, NZ, TOK, FEAT), BF16),
            pltpu.VMEM((NY * NZ * TOK, FEAT), BF16),
            pltpu.VMEM((NY * NZ * TOK, FEAT), BF16),
            pltpu.VMEM((FEAT, 2 * HID), BF16),
            pltpu.VMEM((HID, FEAT), BF16),
            pltpu.VMEM((NX, NC, GROUP, 2 * HID), F32),
            pltpu.VMEM((NX, GROUP, 2 * HID), F32),
            pltpu.VMEM((NX, GROUP, 2 * HID), F32),
            pltpu.VMEM((NX, GROUP, 2 * HID), F32),
            pltpu.VMEM((NX, NC, GROUP, HID), F32),
            pltpu.VMEM((NX, GROUP, HID), F32),
            pltpu.VMEM((NX, GROUP, HID), F32),
            pltpu.VMEM((NX, GROUP, HID), F32),
            pltpu.VMEM((NX, NC, GROUP, HID), BF16),
            pltpu.VMEM((NX, NC, GROUP, 2 * HID), BF16),
            pltpu.VMEM((NY, 2 * GROUP, FEAT), BF16),
            pltpu.VMEM((NY, 2 * GROUP, FEAT), BF16),
            pltpu.VMEM((2 * GROUP, FEAT), F32),
            pltpu.VMEM((11, TOK, FEAT), BF16),
            pltpu.VMEM((5, TOK, FEAT), BF16),
            pltpu.VMEM((5, TOK, FEAT), BF16),
            pltpu.VMEM((1, TOK, FEAT), BF16),
            pltpu.VMEM((4, TOK, FEAT), BF16),
            pltpu.VMEM((4, TOK, FEAT), BF16),
            pltpu.VMEM((FEAT, 2 * HID), BF16),
            pltpu.VMEM((HID, FEAT), BF16),
            pltpu.SemaphoreType.DMA((N_SENDS,)),
            pltpu.SemaphoreType.DMA((N_SENDS,)),
            pltpu.SemaphoreType.DMA((N_LOADS,)),
        ],
        compiler_params=pltpu.CompilerParams(
            collective_id=0, has_side_effects=True, vmem_limit_bytes=48 << 20
        ),
        cost_estimate=pl.CostEstimate(
            flops=16 * NY * NZ * TOK * FEAT * HID, bytes_accessed=12 * FEAT * HID, transcendentals=0
        ),
    )(activations, gate_weight, up_weight, down_weight, out_grad)
    return grad_input, grad_gate, grad_up, grad_down


def solution(mesh):
    placed = (P("row", "col"), P("col", "row"), P("col", "row"), P("row", "col"), P("row", "col"))
    return jax.shard_map(
        on_device,
        mesh=mesh,
        in_specs=placed,
        out_specs=(P("row", "col"), P("col", "row"), P("col", "row"), P("row", "col")),
        check_vma=False,
    )
```

time: 1080 us -> 94.5 us (0.09)
  waiting for transfers between devices: 1050 us -> 0 us
  Pallas kernels: 0 us -> 85.9 us
  between operations: 13.8 us -> 0.65 us
  matrix products: 12 us -> 0 us
    reduce_scatter x1 -> x0, waiting for transfers between devices: 692 us -> none  [on_device(): lax.psum_scatter(contract_cols(grad_gate, gate_weight) + contract_cols(gr...]
    all_gather x2 -> x0, waiting for transfers between devices: 280 us -> none  [the longest x1 146 us: on_device(): input_cols = lax.all_gather(activations, 'row', axis=0, tiled=True)]
    pallas_call x0 -> x1, Pallas kernels: none -> 85.9 us  [on_device(): pl.pallas_call(kernel, out_shape=(jax.ShapeDtypeStruct((TOK, FEAT), F32),...]
    psum x1 -> x0, waiting for transfers between devices: 73.9 us -> none  [on_device(): pre_gate, pre_up = lax.psum((gate_part, up_part), 'col')]
    dot_general x8 -> x0, matrix products: 12 us -> none  [the longest x3 4.77 us: contract_cols(): lax.dot_general(left, right, (((1,), (1,)), ((), ())), preferred_element_...]
  transfers between devices with their start and end apart: 4 -> 0, of which waited for: 4 -> 0; matrix products, arithmetic and copies ran while one was open for 1% -> 0% of each run, Pallas kernels for 0% -> 0%
where the time goes in v1:
time: 94.5 us; the launch traced here: 94.1 us
  Pallas kernels  85.9 us (91%)
  local copies, waits for them, and re-layouts  7.55 us (8%)
    pallas_call x1, Pallas kernels, on_device(): pl.pallas_call(kernel, out_shape=(jax.ShapeDtypeStruct((TOK, FEAT), F32),...  85.9 us
    unnamed x14, local copies, waits for them, and re-layouts  7.55 us

profile of v1, /device:TPU:6, one launch (start us, length us, event | category | flops | bytes accessed | tf_op | source)
XLA Modules:
  0.0 94.1 jit_solution(14078191955287075038)
XLA Ops:
  0.6 0.0 copy-start
  0.6 1.0 %copy-done = bf16[1024,256]{1,0:T(8,128)(2,1)S(1)} copy-done((bf16[1024,256]{1,0:T(8,128)(2,1)S(1)}, bf16[1024,256]{1,0:T(8,128)(2,1)}, u32[]{:S(2)}) %copy-start) | copy-done | bytes 524312
  1.7 0.0 copy-start.1
  1.7 1.0 %copy-done.1 = bf16[1024,256]{1,0:T(8,128)(2,1)S(1)} copy-done((bf16[1024,256]{1,0:T(8,128)(2,1)S(1)}, bf16[1024,256]{1,0:T(8,128)(2,1)}, u32[]{:S(2)}) %copy-start.1) | copy-done | bytes 524312
  2.7 0.0 copy-start.2
  2.7 1.0 %copy-done.2 = bf16[256,1024]{1,0:T(8,128)(2,1)S(1)} copy-done((bf16[256,1024]{1,0:T(8,128)(2,1)S(1)}, bf16[256,1024]{1,0:T(8,128)(2,1)}, u32[]{:S(2)}) %copy-start.2) | copy-done | bytes 524312
  3.8 0.0 copy-start.3
  3.8 0.7 copy-done.3
  4.5 0.0 copy-start.4
  4.5 0.7 copy-done.4
  5.2 85.9 %shard_map.84 = (f32[8,1024]{1,0:T(8,128)S(1)}, bf16[1024,256]{1,0:T(8,128)(2,1)S(1)}, bf16[1024,256]{1,0:T(8,128)(2,1)S(1)}, bf16[256,1024]{1,0:T(8,128)(2,1)S(1)}) custom-call(bf16[8,1024]{1,0:T(8,128)(2,1)S(1)} %copy-done.3, bf16[1024,256]{1,0:T(8,128)(2,1)S(1)} %copy-done, bf16[1024,256]{1,0:T(8,128)(2,1)S(1)} %copy-done.1, ...), custom_call_target="tpu_custom_call" | custom-call | flops 2147483648 | bytes 3145728 | tf_op jit(solution)/shard_map/pallas_call | solution.py:241
  91.1 0.6 copy.13
  91.7 0.8 copy.14
  92.5 0.8 copy.15
  93.3 0.8 copy.16
Async XLA Ops:
  0.6 1.0 %copy-start = (bf16[1024,256]{1,0:T(8,128)(2,1)S(1)}, bf16[1024,256]{1,0:T(8,128)(2,1)}, u32[]{:S(2)}) copy-start(bf16[1024,256]{1,0:T(8,128)(2,1)} %wg_in.1) | copy-start | bytes 1572868
  1.7 1.0 %copy-start.1 = (bf16[1024,256]{1,0:T(8,128)(2,1)S(1)}, bf16[1024,256]{1,0:T(8,128)(2,1)}, u32[]{:S(2)}) copy-start(bf16[1024,256]{1,0:T(8,128)(2,1)} %wu_in.1) | copy-start | bytes 1572868
  2.7 1.0 %copy-start.2 = (bf16[256,1024]{1,0:T(8,128)(2,1)S(1)}, bf16[256,1024]{1,0:T(8,128)(2,1)}, u32[]{:S(2)}) copy-start(bf16[256,1024]{1,0:T(8,128)(2,1)} %wd_in.1) | copy-start | bytes 1572868
  3.8 0.7 copy-start.3
  4.5 0.7 copy-start.4

commit v2 on v0

v2 whole, which is shorter than its diff:
```python
import functools

import jax
import jax.numpy as jnp
from jax import lax
from jax.experimental import pallas as pl
from jax.experimental.pallas import tpu as pltpu
from jax.sharding import PartitionSpec as P

MESH = pl.DeviceIdType.MESH
F32, BF16 = jnp.float32, jnp.bfloat16
NY, NZ, NX, NC = 4, 16, 4, 2
TOK, HID, FEAT = 8, 256, 1024
LEFT, RIGHT = 640, 384
SLOTS = NZ // 2
GROUP = SLOTS * TOK // NC
ROWS = NY * SLOTS * TOK
WIDE = 3 * HID


def contract_cols(left, right):
    return lax.dot_general(left, right, (((1,), (1,)), ((), ())), preferred_element_type=F32)


def contract_rows(left, right):
    return lax.dot_general(left, right, (((0,), (0,)), ((), ())), preferred_element_type=F32)


def kernel(
    x_in, wg_in, wu_in, wd_in, dy_in,
    gi_out, gw_out, uw_out, dw_out,
    t, xm, dm, w2, wd,
    part, r1, s, r2, hg,
    gs, yr, acc1, acc2, nb1, nra1, nrb1, nrc1, nb2, nra2, nrb2, nrc2, ty, tr, tot, cs, cr,
    gw2, dwd,
    send_sem, recv_sem, load_sem,
):
    row, col = lax.axis_index("row"), lax.axis_index("col")
    y, z = row // NZ, row % NZ
    x, c = col // NC, col % NC
    o = 1 - c

    def at(dy=0, dz=0, dx=0):
        return (
            ((y + dy + NY) % NY) * NZ + (z + dz + NZ) % NZ,
            ((x + dx + NX) % NX) * NC + c,
        )

    other = (row, x * NC + o)

    loads = []

    def load(src, dst):
        copy = pltpu.make_async_copy(src, dst, load_sem.at[len(loads)])
        copy.start()
        loads.append(copy)
        return copy

    own = [load(x_in, t.at[0, 0, 0]), load(dy_in, t.at[1, 0, 0])]
    weights = [
        load(wg_in, w2.at[:, pl.ds(0, HID)]),
        load(wu_in, w2.at[:, pl.ds(HID, HID)]),
        load(wd_in, wd),
    ]

    peers = [at(dz=k) for k in (1, -1, 2, -2, 3, -3, 6, -6)]
    peers += [at(dy=k) for k in (1, -1, 2)] + [at(dx=k) for k in (1, -1, 2)] + [other]
    barrier = pltpu.get_barrier_semaphore()
    for peer in peers:
        pl.semaphore_signal(barrier, inc=1, device_id=peer, device_id_type=MESH)
    for copy in own:
        copy.wait()
    pl.semaphore_wait(barrier, len(peers))

    sent = []

    def send(src, dst, to):
        i = len(sent)
        copy = pltpu.make_async_remote_copy(
            src_ref=src, dst_ref=dst, send_sem=send_sem.at[i], recv_sem=recv_sem.at[i],
            device_id=to, device_id_type=MESH,
        )
        copy.start()
        sent.append(copy)
        return copy

    def arrived(copies):
        for copy in copies:
            copy.wait_recv()

    def spread(which, slots):
        return [send(t.at[which, 0, slots], t.at[which, NY - k, slots], at(dy=k)) for k in (2, 1, 3)]

    def near(which, ys, start, size):
        def to(offset):
            return t.at[which, ys, pl.ds(offset + start, size)]

        return [send(to(0), to(5), at(dz=1)), send(to(0), to(10), at(dz=-1))]

    def near_last(which, ys):
        return near(which, ys, 3, 2) + [
            send(t.at[which, ys, pl.ds(3, 1)], t.at[which, ys, pl.ds(15, 1)], at(dz=-2))
        ]

    both, acts, grads = slice(None), 0, 1
    first, all_y = pl.ds(0, 1), slice(None)
    far = []
    for i, k in ((2, 3), (1, -3)):
        far.append(send(t.at[:, 0, 0], t.at[:, 0, i], at(dz=k)))
    near0 = near(acts, first, 0, 1)
    early0 = spread(both, pl.ds(0, 1))
    arrived(near0)
    late0 = spread(acts, pl.ds(5, 1))
    late1 = spread(acts, pl.ds(10, 1))
    arrived(far[:2])
    far += [send(t.at[:, 0, 2], t.at[:, 0, 4], at(dz=3)), send(t.at[:, 0, 1], t.at[:, 0, 3], at(dz=-3))]
    near1 = near(acts, first, 1, 2)
    early1 = spread(both, pl.ds(1, 2))
    arrived(early0)
    grad_near0 = near(grads, all_y, 0, 1)
    arrived(far[2:])
    near2 = near_last(acts, first)
    early2 = spread(both, pl.ds(3, 2))
    arrived(near1)
    late0 += spread(acts, pl.ds(6, 2))
    late1 += spread(acts, pl.ds(11, 2))
    arrived(early1)
    grad_near1 = near(grads, all_y, 1, 2)
    arrived(near2)
    late1 += spread(acts, pl.ds(8, 2)) + spread(acts, pl.ds(13, 3))
    arrived(early2)
    grad_near2 = near_last(grads, all_y)
    for copy in weights:
        copy.wait()

    def compact(src, dst, half):
        for i in range(2 * NY):
            slab = t[src, i // 2, pl.ds(half * SLOTS + i % 2 * 4, 4)].astype(F32).reshape(4 * TOK, FEAT)
            dst[pl.ds(half * ROWS + i * 4 * TOK, 4 * TOK), :] = slab.astype(BF16)

    def reduce_parts(half):
        rows = pl.ds(half * ROWS, ROWS)
        compact(acts, xm, half)
        compact(grads, dm, half)
        pre = jnp.dot(xm[rows, :], w2[...], preferred_element_type=F32)
        part[half, :, :, :, pl.ds(0, 2 * HID)] = pre.reshape(NX, NC, GROUP, 2 * HID)
        part[half, :, :, :, pl.ds(2 * HID, HID)] = contract_cols(dm[rows, :], wd[...]).reshape(NX, NC, GROUP, HID)
        arrived([send(part.at[half, :, o], r1.at[half], other)])
        over_x = []
        for k in (2, 1, 3, 0):
            m = (x + k) % NX
            s[half, k] = part[half, m, c] + r1[half, m]
            if k:
                over_x.append(send(s.at[half, k], r2.at[half, k], at(dx=k)))
        return over_x

    grad_part, hid_part = pl.ds(0, 2 * HID), pl.ds(2 * HID, HID)

    def activate(half, over_x):
        arrived(over_x)
        total = s[half, 0] + r2[half, 1] + r2[half, 2] + r2[half, 3]
        pre_gate, pre_up, grad_hidden = total[:, :HID], total[:, HID : 2 * HID], total[:, 2 * HID :]
        sigma = jax.nn.sigmoid(pre_gate)
        silu = pre_gate * sigma
        grad_gate = grad_hidden * pre_up * sigma * (1.0 + pre_gate * (1.0 - sigma))
        hg[half, x, c, :, pl.ds(0, HID)] = grad_gate.astype(BF16)
        hg[half, x, c, :, pl.ds(HID, HID)] = (grad_hidden * silu).astype(BF16)
        hg[half, x, c, :, pl.ds(2 * HID, HID)] = (silu * pre_up).astype(BF16)
        mine = hg.at[half, x, c]
        return [
            [send(mine.at[:, what], mine.at[:, what], at(dx=k)) for k in (2, 1, 3)] for what in (grad_part, hid_part)
        ]

    def pass_on(half, copies, what):
        arrived(copies)
        mine = hg.at[half, :, c, :, what]
        return [send(mine, mine, other)]

    arrived(late0)
    arrived(grad_near0[:1] + grad_near1[:1])
    over_x0 = reduce_parts(0)
    arrived(late1)
    arrived(grad_near0[1:] + grad_near1[1:] + grad_near2)
    over_x1 = reduce_parts(1)
    gathered0 = activate(0, over_x0)
    gathered1 = activate(1, over_x1)
    def input_grad(half, columns):
        product = contract_cols(hg[half, :, :, :, : 2 * HID].reshape(ROWS, 2 * HID), w2[columns, :])
        return product.reshape(NY, SLOTS, TOK, product.shape[-1])

    def send_near(block, a, b, c):
        return [send(block[0], a, at(dz=-1)), send(block[1], b, at(dz=1)), send(block[2], c, at(dz=2))]

    left_y, right_near = [], []
    for half, gathered in enumerate((gathered0, gathered1)):
        arrived(pass_on(half, gathered[0], grad_part))
        rows = pl.ds(half * SLOTS * TOK, SLOTS * TOK)
        grad = input_grad(half, slice(0, LEFT)).reshape(NY, SLOTS * TOK, LEFT)
        for k in (2, 1, 3):
            gs[k, rows] = grad[k].astype(BF16)
            left_y.append(send(gs.at[k, rows], yr.at[k, rows], at(dy=k)))
        acc1[rows, :] = grad[0]
        grad = input_grad(half, slice(LEFT, FEAT))
        if half == 0:
            acc2[...] = grad[:, :5]
            nb2[:, pl.ds(0, 3)] = grad[:, 5:].astype(BF16)
            right_near.append(send(nb2.at[:, pl.ds(0, 3)], nra2.at[:, pl.ds(0, 3)], at(dz=-1)))
        else:
            nb2[:, pl.ds(3, 8)] = grad.astype(BF16)
            right_near.append(send(nb2.at[:, pl.ds(5, 5)], nrb2, at(dz=1)))
            right_near.append(send(nb2.at[:, pl.ds(3, 2)], nra2.at[:, pl.ds(3, 2)], at(dz=-1)))
            right_near.append(send(nb2.at[:, pl.ds(10, 1)], nrc2, at(dz=2)))

    outs = []
    arrived(pass_on(0, gathered0[1], hid_part) + pass_on(1, gathered1[1], hid_part))
    dwd[...] = contract_rows(hg[:, :, :, :, 2 * HID :].reshape(2 * ROWS, HID), dm[...]).astype(BF16)
    outs.append(load(dwd, dw_out))
    gw2[...] = contract_rows(xm[...], hg[:, :, :, :, : 2 * HID].reshape(2 * ROWS, 2 * HID)).astype(BF16)
    outs.append(load(gw2.at[:, pl.ds(0, HID)], gw_out))
    outs.append(load(gw2.at[:, pl.ds(HID, HID)], uw_out))

    arrived(right_near)
    right_y = []
    for k in (2, 1, 3, 0):
        acc2[k] += nra2[k].astype(F32) + nrb2[k].astype(F32)
        acc2[k, 3] += nrc2[k, 0].astype(F32)
        if k:
            ty[k] = acc2[k].astype(BF16)
            right_y.append(send(ty.at[k], tr.at[k], at(dy=k)))

    arrived(left_y)
    total = acc1[...] + yr[1].astype(F32) + yr[2].astype(F32) + yr[3].astype(F32)
    acc1[...] = total
    nb1[...] = total[5 * TOK :].reshape(11, TOK, LEFT).astype(BF16)
    left_near = send_near([nb1.at[pl.ds(0, 5)], nb1.at[pl.ds(5, 5)], nb1.at[pl.ds(10, 1)]], nra1, nrb1, nrc1)
    left, right = pl.ds(0, LEFT), pl.ds(LEFT, RIGHT)
    arrived(right_y)
    tot[:, :, right] = acc2[0] + tr[1].astype(F32) + tr[2].astype(F32) + tr[3].astype(F32)
    arrived(left_near)
    tot[:, :, left] = acc1[: 5 * TOK].reshape(5, TOK, LEFT) + nra1[...].astype(F32) + nrb1[...].astype(F32)
    tot[3, :, left] += nrc1[0].astype(F32)

    far = []
    for i, k in ((3, 6), (4, -6), (1, 3), (2, -3)):
        cs[i] = tot[i].astype(BF16)
        far.append(send(cs.at[i], cr.at[i], at(dz=k)))
    arrived(far)
    gi_out[...] = tot[0] + cr[1].astype(F32) + cr[2].astype(F32) + cr[3].astype(F32) + cr[4].astype(F32)

    for copy in outs:
        copy.wait()
    for copy in sent:
        copy.wait_send()


def write_out(*refs):
    copies = [pltpu.make_async_copy(refs[i], refs[4 + i], refs[8].at[i]) for i in range(4)]
    for copy in copies:
        copy.start()
    for copy in copies:
        copy.wait()


N_SENDS = 96
N_LOADS = 8


def on_device(activations, gate_weight, up_weight, down_weight, out_grad):
    anywhere = pl.BlockSpec(memory_space=pl.ANY)
    hbm = pl.BlockSpec(memory_space=pltpu.HBM)
    vmem = pl.BlockSpec(memory_space=pltpu.VMEM)
    results = pl.pallas_call(
        kernel,
        out_shape=(
            jax.ShapeDtypeStruct((TOK, FEAT), F32),
            jax.ShapeDtypeStruct((FEAT, HID), BF16),
            jax.ShapeDtypeStruct((FEAT, HID), BF16),
            jax.ShapeDtypeStruct((HID, FEAT), BF16),
        ),
        in_specs=[hbm] * 5,
        out_specs=(vmem, anywhere, anywhere, anywhere),
        scratch_shapes=[
            pltpu.VMEM((2, NY, NZ, TOK, FEAT), BF16),
            pltpu.VMEM((2 * ROWS, FEAT), BF16),
            pltpu.VMEM((2 * ROWS, FEAT), BF16),
            pltpu.VMEM((FEAT, 2 * HID), BF16),
            pltpu.VMEM((HID, FEAT), BF16),
            pltpu.VMEM((2, NX, NC, GROUP, WIDE), F32),
            pltpu.VMEM((2, NX, GROUP, WIDE), F32),
            pltpu.VMEM((2, NX, GROUP, WIDE), F32),
            pltpu.VMEM((2, NX, GROUP, WIDE), F32),
            pltpu.VMEM((2, NX, NC, GROUP, WIDE), BF16),
            pltpu.VMEM((NY, NZ * TOK, LEFT), BF16),
            pltpu.VMEM((NY, NZ * TOK, LEFT), BF16),
            pltpu.VMEM((NZ * TOK, LEFT), F32),
            pltpu.VMEM((NY, 5, TOK, RIGHT), F32),
            pltpu.VMEM((11, TOK, LEFT), BF16),
            pltpu.VMEM((5, TOK, LEFT), BF16),
            pltpu.VMEM((5, TOK, LEFT), BF16),
            pltpu.VMEM((1, TOK, LEFT), BF16),
            pltpu.VMEM((NY, 11, TOK, RIGHT), BF16),
            pltpu.VMEM((NY, 5, TOK, RIGHT), BF16),
            pltpu.VMEM((NY, 5, TOK, RIGHT), BF16),
            pltpu.VMEM((NY, 1, TOK, RIGHT), BF16),
            pltpu.VMEM((NY, 5, TOK, RIGHT), BF16),
            pltpu.VMEM((NY, 5, TOK, RIGHT), BF16),
            pltpu.VMEM((5, TOK, FEAT), F32),
            pltpu.VMEM((5, TOK, FEAT), BF16),
            pltpu.VMEM((5, TOK, FEAT), BF16),
            pltpu.VMEM((FEAT, 2 * HID), BF16),
            pltpu.VMEM((HID, FEAT), BF16),
            pltpu.SemaphoreType.DMA((N_SENDS,)),
            pltpu.SemaphoreType.DMA((N_SENDS,)),
            pltpu.SemaphoreType.DMA((N_LOADS,)),
        ],
        compiler_params=pltpu.CompilerParams(
            collective_id=0, has_side_effects=True, vmem_limit_bytes=62 << 20
        ),
        cost_estimate=pl.CostEstimate(
            flops=16 * NY * NZ * TOK * FEAT * HID, bytes_accessed=12 * FEAT * HID, transcendentals=0
        ),
    )(activations, gate_weight, up_weight, down_weight, out_grad)
    return pl.pallas_call(
        write_out,
        out_shape=tuple(jax.ShapeDtypeStruct(r.shape, r.dtype) for r in results),
        in_specs=[vmem] * 4,
        out_specs=(hbm,) * 4,
        scratch_shapes=[pltpu.SemaphoreType.DMA((4,))],
    )(*results)


def solution(mesh):
    placed = (P("row", "col"), P("col", "row"), P("col", "row"), P("row", "col"), P("row", "col"))
    return jax.shard_map(
        on_device,
        mesh=mesh,
        in_specs=placed,
        out_specs=(P("row", "col"), P("col", "row"), P("col", "row"), P("row", "col")),
        check_vma=False,
    )
```

time: 1080 us -> 74.5 us (0.07)
  waiting for transfers between devices: 1050 us -> 0 us
  Pallas kernels: 0 us -> 73.7 us
  between operations: 13.8 us -> 0.64 us
  matrix products: 12 us -> 0 us
    reduce_scatter x1 -> x0, waiting for transfers between devices: 692 us -> none  [on_device(): lax.psum_scatter(contract_cols(grad_gate, gate_weight) + contract_cols(gr...]
    all_gather x2 -> x0, waiting for transfers between devices: 280 us -> none  [the longest x1 146 us: on_device(): input_cols = lax.all_gather(activations, 'row', axis=0, tiled=True)]
    psum x1 -> x0, waiting for transfers between devices: 73.9 us -> none  [on_device(): pre_gate, pre_up = lax.psum((gate_part, up_part), 'col')]
    pallas_call x0 -> x2, Pallas kernels: none -> 73.7 us  [the longest x1 71.1 us: on_device(): pl.pallas_call(kernel, out_shape=(jax.ShapeDtypeStruct((TOK, FEAT), F32),...]
    dot_general x8 -> x0, matrix products: 12 us -> none  [the longest x3 4.77 us: contract_cols(): lax.dot_general(left, right, (((1,), (1,)), ((), ())), preferred_element_...]
  transfers between devices with their start and end apart: 4 -> 0, of which waited for: 4 -> 0; matrix products, arithmetic and copies ran while one was open for 1% -> 0% of each run, Pallas kernels for 0% -> 0%
where the time goes in v2:
time: 74.5 us; the launch traced here: 74.3 us
  Pallas kernels  73.7 us (99%)
    pallas_call x1, Pallas kernels, on_device(): pl.pallas_call(kernel, out_shape=(jax.ShapeDtypeStruct((TOK, FEAT), F32),...  71.1 us
    pallas_call x1, Pallas kernels, on_device(): pl.pallas_call(write_out, out_shape=tuple((jax.ShapeDtypeStruct(r.shape,...  2.56 us

profile of v2, /device:TPU:6, one launch (start us, length us, event | category | flops | bytes accessed | tf_op | source)
XLA Modules:
  0.0 74.3 jit_solution(9018166037531901768)
XLA Ops:
  0.6 71.1 %shard_map.84 = (f32[8,1024]{1,0:T(8,128)}, bf16[1024,256]{1,0:T(8,128)(2,1)}, bf16[1024,256]{1,0:T(8,128)(2,1)}, bf16[256,1024]{1,0:T(8,128)(2,1)}) custom-call(bf16[8,1024]{1,0:T(8,128)(2,1)} %x_in.1, bf16[1024,256]{1,0:T(8,128)(2,1)} %wg_in.1, bf16[1024,256]{1,0:T(8,128)(2,1)} %wu_in.1, bf16[256,1024]{1,0:T(8,128)(2,1)} %wd_in.1, bf16[8,1024]{1,0:T(8,128)(2,1)} %dy_in.1), custom_call_target="tpu_custom_call" | custom-call | flops 2147483648 | bytes 3145728 | tf_op jit(solution)/shard_map/pallas_call | solution.py:272
  71.8 2.6 %shard_map.85 = (f32[8,1024]{1,0:T(8,128)}, bf16[1024,256]{1,0:T(8,128)(2,1)}, bf16[1024,256]{1,0:T(8,128)(2,1)}, bf16[256,1024]{1,0:T(8,128)(2,1)}) custom-call(f32[8,1024]{1,0:T(8,128)} %get-tuple-element.8.refs_0_, bf16[1024,256]{1,0:T(8,128)(2,1)} %get-tuple-element.9.refs_1_, bf16[1024,256]{1,0:T(8,128)(2,1)} %get-tuple-element.10.refs_2_, ...), custom_call_target="tpu_custom_call" | custom-call | tf_op jit(solution)/shard_map/pallas_call | solution.py:323

commit v3 on v2

--- a/solution.py
+++ b/solution.py
@@ -30,7 +30,7 @@
     x_in, wg_in, wu_in, wd_in, dy_in,
     gi_out, gw_out, uw_out, dw_out,
     t, xm, dm, w2, wd,
-    part, r1, s, r2, hg,
+    part, r1, s, s16, r2, hg,
     gs, yr, acc1, acc2, nb1, nra1, nrb1, nrc1, nb2, nra2, nrb2, nrc2, ty, tr, tot, cs, cr,
     gw2, dwd,
     send_sem, recv_sem, load_sem,
@@ -63,7 +63,7 @@
         load(wd_in, wd),
     ]
 
-    peers = [at(dz=k) for k in (1, -1, 2, -2, 3, -3, 6, -6)]
+    peers = [at(dz=k) for k in (1, -1, 2, -2, 3, -3)]
     peers += [at(dy=k) for k in (1, -1, 2)] + [at(dx=k) for k in (1, -1, 2)] + [other]
     barrier = pltpu.get_barrier_semaphore()
     for peer in peers:
@@ -149,16 +149,19 @@
         over_x = []
         for k in (2, 1, 3, 0):
             m = (x + k) % NX
-            s[half, k] = part[half, m, c] + r1[half, m]
+            value = part[half, m, c] + r1[half, m]
             if k:
-                over_x.append(send(s.at[half, k], r2.at[half, k], at(dx=k)))
+                s16[half, k] = value.astype(BF16)
+                over_x.append(send(s16.at[half, k], r2.at[half, k], at(dx=k)))
+            else:
+                s[half] = value
         return over_x
 
     grad_part, hid_part = pl.ds(0, 2 * HID), pl.ds(2 * HID, HID)
 
     def activate(half, over_x):
         arrived(over_x)
-        total = s[half, 0] + r2[half, 1] + r2[half, 2] + r2[half, 3]
+        total = s[half] + r2[half, 1].astype(F32) + r2[half, 2].astype(F32) + r2[half, 3].astype(F32)
         pre_gate, pre_up, grad_hidden = total[:, :HID], total[:, HID : 2 * HID], total[:, 2 * HID :]
         sigma = jax.nn.sigmoid(pre_gate)
         silu = pre_gate * sigma
@@ -254,13 +257,26 @@
 
 
 def write_out(*refs):
-    copies = [pltpu.make_async_copy(refs[i], refs[4 + i], refs[8].at[i]) for i in range(4)]
-    for copy in copies:
+    sources, results, (small, wide, load_sem, store_sem) = refs[:4], refs[4:8], refs[8:]
+    pieces = [(sources[0], small, results[0])]
+    for i in range(1, 4):
+        rows = sources[i].shape[0] // CHUNKS
+        for j in range(CHUNKS):
+            piece = pl.ds(j * rows, rows)
+            held = wide[i - 1].at[piece]
+            pieces.append((sources[i].at[piece], held, results[i].at[piece]))
+    loads = [pltpu.make_async_copy(a, b, load_sem.at[n]) for n, (a, b, _) in enumerate(pieces)]
+    stores = [pltpu.make_async_copy(b, c, store_sem.at[n]) for n, (_, b, c) in enumerate(pieces)]
+    for copy in loads:
         copy.start()
-    for copy in copies:
-        copy.wait()
-
-
+    for i, copy in enumerate(loads):
+        copy.wait()
+        stores[i].start()
+    for copy in stores:
+        copy.wait()
+
+
+CHUNKS = 2
 N_SENDS = 96
 N_LOADS = 8
 
@@ -287,8 +303,9 @@
             pltpu.VMEM((HID, FEAT), BF16),
             pltpu.VMEM((2, NX, NC, GROUP, WIDE), F32),
             pltpu.VMEM((2, NX, GROUP, WIDE), F32),
-            pltpu.VMEM((2, NX, GROUP, WIDE), F32),
-            pltpu.VMEM((2, NX, GROUP, WIDE), F32),
+            pltpu.VMEM((2, GROUP, WIDE), F32),
+            pltpu.VMEM((2, NX, GROUP, WIDE), BF16),
+            pltpu.VMEM((2, NX, GROUP, WIDE), BF16),
             pltpu.VMEM((2, NX, NC, GROUP, WIDE), BF16),
             pltpu.VMEM((NY, NZ * TOK, LEFT), BF16),
             pltpu.VMEM((NY, NZ * TOK, LEFT), BF16),
@@ -323,9 +340,15 @@
     return pl.pallas_call(
         write_out,
         out_shape=tuple(jax.ShapeDtypeStruct(r.shape, r.dtype) for r in results),
-        in_specs=[vmem] * 4,
+        in_specs=[hbm] * 4,
         out_specs=(hbm,) * 4,
-        scratch_shapes=[pltpu.SemaphoreType.DMA((4,))],
+        scratch_shapes=[
+            pltpu.VMEM((TOK, FEAT), F32),
+            [pltpu.VMEM(r.shape, BF16) for r in results[1:]],
+            pltpu.SemaphoreType.DMA((1 + 3 * CHUNKS,)),
+            pltpu.SemaphoreType.DMA((1 + 3 * CHUNKS,)),
+        ],
+        compiler_params=pltpu.CompilerParams(vmem_limit_bytes=62 << 20),
     )(*results)
 
 

time: 74.5 us -> 69.4 us (0.932); the launches traced: 74.3 us -> 68.2 us
  Pallas kernels: 73.7 us -> 67.6 us
    pallas_call x1, Pallas kernels: 71.1 us -> 65.4 us  [on_device(): pl.pallas_call(kernel, out_shape=(jax.ShapeDtypeStruct((TOK, FEAT), F32),...]
where the time goes in v3:
time: 69.4 us; the launch traced here: 68.2 us
  Pallas kernels  67.6 us (97%)
    pallas_call x1, Pallas kernels, on_device(): pl.pallas_call(kernel, out_shape=(jax.ShapeDtypeStruct((TOK, FEAT), F32),...  65.4 us
    pallas_call x1, Pallas kernels, on_device(): pl.pallas_call(write_out, out_shape=tuple((jax.ShapeDtypeStruct(r.shape,...  2.23 us

profile of v3, /device:TPU:6, one launch (start us, length us, event | category | flops | bytes accessed | tf_op | source)
XLA Modules:
  0.0 68.2 jit_solution(17762046434109666624)
XLA Ops:
  0.6 65.4 %shard_map.84 = (f32[8,1024]{1,0:T(8,128)}, bf16[1024,256]{1,0:T(8,128)(2,1)}, bf16[1024,256]{1,0:T(8,128)(2,1)}, bf16[256,1024]{1,0:T(8,128)(2,1)}) custom-call(bf16[8,1024]{1,0:T(8,128)(2,1)} %x_in.1, bf16[1024,256]{1,0:T(8,128)(2,1)} %wg_in.1, bf16[1024,256]{1,0:T(8,128)(2,1)} %wu_in.1, bf16[256,1024]{1,0:T(8,128)(2,1)} %wd_in.1, bf16[8,1024]{1,0:T(8,128)(2,1)} %dy_in.1), custom_call_target="tpu_custom_call" | custom-call | flops 2147483648 | bytes 3145728 | tf_op jit(solution)/shard_map/pallas_call | solution.py:288
  66.0 2.2 %shard_map.85 = (f32[8,1024]{1,0:T(8,128)}, bf16[1024,256]{1,0:T(8,128)(2,1)}, bf16[1024,256]{1,0:T(8,128)(2,1)}, bf16[256,1024]{1,0:T(8,128)(2,1)}) custom-call(f32[8,1024]{1,0:T(8,128)} %get-tuple-element.8.refs_0_, bf16[1024,256]{1,0:T(8,128)(2,1)} %get-tuple-element.9.refs_1_, bf16[1024,256]{1,0:T(8,128)(2,1)} %get-tuple-element.10.refs_2_, ...), custom_call_target="tpu_custom_call" | custom-call | tf_op jit(solution)/shard_map/pallas_call | solution.py:340

commit v4 on v3

--- a/solution.py
+++ b/solution.py
@@ -40,13 +40,23 @@
     x, c = col // NC, col % NC
     o = 1 - c
 
+    places = {}
+
     def at(dy=0, dz=0, dx=0):
-        return (
-            ((y + dy + NY) % NY) * NZ + (z + dz + NZ) % NZ,
-            ((x + dx + NX) % NX) * NC + c,
-        )
+        if (dy, dz, dx) not in places:
+            places[dy, dz, dx] = (
+                ((y + dy + NY) % NY) * NZ + (z + dz + NZ) % NZ,
+                ((x + dx + NX) % NX) * NC + c,
+            )
+        return places[dy, dz, dx]
 
     other = (row, x * NC + o)
+
+    peers = [at(dz=k) for k in (3, -3)] + [at(dy=k) for k in (2, 1, -1)] + [at(dz=k) for k in (2, -2, 1, -1)]
+    peers += [at(dx=k) for k in (2, 1, -1)] + [other]
+    barrier = pltpu.get_barrier_semaphore()
+    for peer in peers:
+        pl.semaphore_signal(barrier, inc=1, device_id=peer, device_id_type=MESH)
 
     loads = []
 
@@ -56,6 +66,7 @@
         loads.append(copy)
         return copy
 
+    at(dz=6), at(dz=-6)
     own = [load(x_in, t.at[0, 0, 0]), load(dy_in, t.at[1, 0, 0])]
     weights = [
         load(wg_in, w2.at[:, pl.ds(0, HID)]),
@@ -63,11 +74,6 @@
         load(wd_in, wd),
     ]
 
-    peers = [at(dz=k) for k in (1, -1, 2, -2, 3, -3)]
-    peers += [at(dy=k) for k in (1, -1, 2)] + [at(dx=k) for k in (1, -1, 2)] + [other]
-    barrier = pltpu.get_barrier_semaphore()
-    for peer in peers:
-        pl.semaphore_signal(barrier, inc=1, device_id=peer, device_id_type=MESH)
     for copy in own:
         copy.wait()
     pl.semaphore_wait(barrier, len(peers))
@@ -126,10 +132,12 @@
     late1 += spread(acts, pl.ds(11, 2))
     arrived(early1)
     grad_near1 = near(grads, all_y, 1, 2)
+    grad_near2 = near(grads, first, 3, 2)
     arrived(near2)
     late1 += spread(acts, pl.ds(8, 2)) + spread(acts, pl.ds(13, 3))
     arrived(early2)
-    grad_near2 = near_last(grads, all_y)
+    grad_near2 += near(grads, pl.ds(1, 3), 3, 2)
+    grad_near2.append(send(t.at[grads, :, 3], t.at[grads, :, 15], at(dz=-2)))
     for copy in weights:
         copy.wait()
 
@@ -138,14 +146,18 @@
             slab = t[src, i // 2, pl.ds(half * SLOTS + i % 2 * 4, 4)].astype(F32).reshape(4 * TOK, FEAT)
             dst[pl.ds(half * ROWS + i * 4 * TOK, 4 * TOK), :] = slab.astype(BF16)
 
-    def reduce_parts(half):
+    def reduce_parts(half, of_grads):
         rows = pl.ds(half * ROWS, ROWS)
+        pre_part, grad_part = pl.ds(0, 2 * HID), pl.ds(2 * HID, HID)
         compact(acts, xm, half)
+        pre = jnp.dot(xm[rows, :], w2[...], preferred_element_type=F32)
+        part[half, :, :, :, pre_part] = pre.reshape(NX, NC, GROUP, 2 * HID)
+        to_other = [send(part.at[half, :, o, :, pre_part], r1.at[half, :, :, pre_part], other)]
+        arrived(of_grads)
         compact(grads, dm, half)
-        pre = jnp.dot(xm[rows, :], w2[...], preferred_element_type=F32)
-        part[half, :, :, :, pl.ds(0, 2 * HID)] = pre.reshape(NX, NC, GROUP, 2 * HID)
-        part[half, :, :, :, pl.ds(2 * HID, HID)] = contract_cols(dm[rows, :], wd[...]).reshape(NX, NC, GROUP, HID)
-        arrived([send(part.at[half, :, o], r1.at[half], other)])
+        part[half, :, :, :, grad_part] = contract_cols(dm[rows, :], wd[...]).reshape(NX, NC, GROUP, HID)
+        to_other.append(send(part.at[half, :, o, :, grad_part], r1.at[half, :, :, grad_part], other))
+        arrived(to_other)
         over_x = []
         for k in (2, 1, 3, 0):
             m = (x + k) % NX
@@ -175,16 +187,18 @@
         ]
 
     def pass_on(half, copies, what):
-        arrived(copies)
-        mine = hg.at[half, :, c, :, what]
-        return [send(mine, mine, other)]
+        mine = hg.at[half, x, c, :, what]
+        crossed = [send(mine, mine, other)]
+        for k, copy in zip((2, 1, 3), copies):
+            arrived([copy])
+            block = hg.at[half, (x - k + NX) % NX, c, :, what]
+            crossed.append(send(block, block, other))
+        return crossed
 
     arrived(late0)
-    arrived(grad_near0[:1] + grad_near1[:1])
-    over_x0 = reduce_parts(0)
+    over_x0 = reduce_parts(0, grad_near0[:1] + grad_near1[:1])
     arrived(late1)
-    arrived(grad_near0[1:] + grad_near1[1:] + grad_near2)
-    over_x1 = reduce_parts(1)
+    over_x1 = reduce_parts(1, grad_near0[1:] + grad_near1[1:] + grad_near2)
     gathered0 = activate(0, over_x0)
     gathered1 = activate(1, over_x1)
     def input_grad(half, columns):
@@ -277,7 +291,7 @@
 
 
 CHUNKS = 2
-N_SENDS = 96
+N_SENDS = 112
 N_LOADS = 8
 
 

time: 69.4 us -> 69.3 us (level)
  the two profiles are of different devices: /device:TPU:6 before, /device:TPU:32 now
where the time goes in v4:
time: 69.3 us; the launch traced here: 69.1 us
  Pallas kernels  68.5 us (99%)
    pallas_call x1, Pallas kernels, on_device(): pl.pallas_call(kernel, out_shape=(jax.ShapeDtypeStruct((TOK, FEAT), F32),...  66.3 us
    pallas_call x1, Pallas kernels, on_device(): pl.pallas_call(write_out, out_shape=tuple((jax.ShapeDtypeStruct(r.shape,...  2.23 us

profile of v4, /device:TPU:32, one launch (start us, length us, event | category | flops | bytes accessed | tf_op | source)
XLA Modules:
  0.0 69.1 jit_solution(15047583551964336497)
XLA Ops:
  0.6 66.3 %shard_map.84 = (f32[8,1024]{1,0:T(8,128)}, bf16[1024,256]{1,0:T(8,128)(2,1)}, bf16[1024,256]{1,0:T(8,128)(2,1)}, bf16[256,1024]{1,0:T(8,128)(2,1)}) custom-call(bf16[8,1024]{1,0:T(8,128)(2,1)} %x_in.1, bf16[1024,256]{1,0:T(8,128)(2,1)} %wg_in.1, bf16[1024,256]{1,0:T(8,128)(2,1)} %wu_in.1, bf16[256,1024]{1,0:T(8,128)(2,1)} %wd_in.1, bf16[8,1024]{1,0:T(8,128)(2,1)} %dy_in.1), custom_call_target="tpu_custom_call" | custom-call | flops 2147483648 | bytes 3145728 | tf_op jit(solution)/shard_map/pallas_call | solution.py:302
  66.9 2.2 %shard_map.85 = (f32[8,1024]{1,0:T(8,128)}, bf16[1024,256]{1,0:T(8,128)(2,1)}, bf16[1024,256]{1,0:T(8,128)(2,1)}, bf16[256,1024]{1,0:T(8,128)(2,1)}) custom-call(f32[8,1024]{1,0:T(8,128)} %get-tuple-element.8.refs_0_, bf16[1024,256]{1,0:T(8,128)(2,1)} %get-tuple-element.9.refs_1_, bf16[1024,256]{1,0:T(8,128)(2,1)} %get-tuple-element.10.refs_2_, ...), custom_call_target="tpu_custom_call" | custom-call | tf_op jit(solution)/shard_map/pallas_call | solution.py:354

commit v5 on v4

--- a/solution.py
+++ b/solution.py
@@ -52,7 +52,7 @@
 
     other = (row, x * NC + o)
 
-    peers = [at(dz=k) for k in (3, -3)] + [at(dy=k) for k in (2, 1, -1)] + [at(dz=k) for k in (2, -2, 1, -1)]
+    peers = [at(dz=k) for k in (3, -3)] + [at(dy=k) for k in (2, 1, -1)] + [at(dz=k) for k in (1, -1)]
     peers += [at(dx=k) for k in (2, 1, -1)] + [other]
     barrier = pltpu.get_barrier_semaphore()
     for peer in peers:
@@ -125,9 +125,10 @@
     arrived(early0)
     grad_near0 = near(grads, all_y, 0, 1)
     arrived(far[2:])
-    near2 = near_last(acts, first)
+    near2 = near(acts, first, 3, 2)
     early2 = spread(both, pl.ds(3, 2))
     arrived(near1)
+    near2.append(send(t.at[acts, first, pl.ds(3, 1)], t.at[acts, first, pl.ds(15, 1)], at(dz=-2)))
     late0 += spread(acts, pl.ds(6, 2))
     late1 += spread(acts, pl.ds(11, 2))
     arrived(early1)

time: 69.3 us -> 69.3 us (level)
  no operation moved by 1% of the time
where the time goes in v5:
time: 69.3 us; the launch traced here: 69.1 us
  Pallas kernels  68.5 us (99%)
    pallas_call x1, Pallas kernels, on_device(): pl.pallas_call(kernel, out_shape=(jax.ShapeDtypeStruct((TOK, FEAT), F32),...  66.2 us
    pallas_call x1, Pallas kernels, on_device(): pl.pallas_call(write_out, out_shape=tuple((jax.ShapeDtypeStruct(r.shape,...  2.23 us

profile of v5, /device:TPU:32, one launch (start us, length us, event | category | flops | bytes accessed | tf_op | source)
XLA Modules:
  0.0 69.1 jit_solution(5129500826794167591)
XLA Ops:
  0.6 66.2 %shard_map.84 = (f32[8,1024]{1,0:T(8,128)}, bf16[1024,256]{1,0:T(8,128)(2,1)}, bf16[1024,256]{1,0:T(8,128)(2,1)}, bf16[256,1024]{1,0:T(8,128)(2,1)}) custom-call(bf16[8,1024]{1,0:T(8,128)(2,1)} %x_in.1, bf16[1024,256]{1,0:T(8,128)(2,1)} %wg_in.1, bf16[1024,256]{1,0:T(8,128)(2,1)} %wu_in.1, bf16[256,1024]{1,0:T(8,128)(2,1)} %wd_in.1, bf16[8,1024]{1,0:T(8,128)(2,1)} %dy_in.1), custom_call_target="tpu_custom_call" | custom-call | flops 2147483648 | bytes 3145728 | tf_op jit(solution)/shard_map/pallas_call | solution.py:303
  66.9 2.2 %shard_map.85 = (f32[8,1024]{1,0:T(8,128)}, bf16[1024,256]{1,0:T(8,128)(2,1)}, bf16[1024,256]{1,0:T(8,128)(2,1)}, bf16[256,1024]{1,0:T(8,128)(2,1)}) custom-call(f32[8,1024]{1,0:T(8,128)} %get-tuple-element.8.refs_0_, bf16[1024,256]{1,0:T(8,128)(2,1)} %get-tuple-element.9.refs_1_, bf16[1024,256]{1,0:T(8,128)(2,1)} %get-tuple-element.10.refs_2_, ...), custom_call_target="tpu_custom_call" | custom-call | tf_op jit(solution)/shard_map/pallas_call | solution.py:355
